TPU v7x, 256 devices: a whole 4x4x8 slice. The times are simulated.
256 devices in a mesh: ty: 16 (over z, core), tx: 16 (over x, y).
Axes of the slice: x: 4, y: 4, z: 8, core: 2. Of those that a mesh axis runs over, the one named last changes fastest.
Arguments:
- object_planes: float32 [2, 2, 4096, 4096], P(None, None, 'ty', 'tx'), may hold values from -5 to 5
- probe: float32 [2, 256, 256], replicated, may hold values from -6 to 6
- positions: int32 [16, 16, 2, 2], P('ty', 'tx'), may hold values from 0 to 255
- measured: float32 [16, 16, 2, 256, 256], P('ty', 'tx'), may hold values from 0.2 to 3
Outputs:
- new_object: float32 [2, 2, 4096, 4096], P(None, None, 'ty', 'tx')
- new_probe: float32 [2, 256, 256], replicated
All inputs are finite; a program needn't handle non-finite values.
Results may differ from a plain program's by a relative error of at most 0.00019.
Values sent between devices are 32-bit elements; how exact they have to be, the bound alone decides.
A program may use at most 128 MiB of HBM per device.

v0:
```python
import math

import jax
import jax.numpy as jnp
from jax import lax
from jax.sharding import PartitionSpec as P

ITERS = 2


def from_behind(shard, axis, by):
    length = lax.axis_size(axis)
    pairs = [(i, i + by) for i in range(length) if 0 <= i + by < length]
    return lax.ppermute(shard, axis, pairs)


def exact_product(left, right):
    return jnp.matmul(
        left, right, precision=lax.Precision.HIGHEST, preferred_element_type=jnp.float32
    )


def dft_tables(size):
    index = jnp.arange(size, dtype=jnp.int32)
    turns = index[:, None] * index[None, :] % size
    angle = 2.0 * math.pi * turns.astype(jnp.float32) / size
    scale = 1.0 / math.sqrt(size)
    return (jnp.cos(angle) * scale, -jnp.sin(angle) * scale)


def fresnel_kernel(size):
    index = jnp.arange(size, dtype=jnp.int32)
    quad = (index[:, None] * index[:, None] + index[None, :] * index[None, :]) % (2 * size)
    phase = -math.pi * quad.astype(jnp.float32) / size
    return (jnp.cos(phase), jnp.sin(phase))


def transform(field_re, field_im, table_re, table_im):
    left_re = exact_product(table_re, field_re) - exact_product(table_im, field_im)
    left_im = exact_product(table_re, field_im) + exact_product(table_im, field_re)
    out_re = exact_product(left_re, table_re) - exact_product(left_im, table_im)
    out_im = exact_product(left_re, table_im) + exact_product(left_im, table_re)
    return (out_re, out_im)


def complex_times(a_re, a_im, b_re, b_im):
    return (a_re * b_re - a_im * b_im, a_re * b_im + a_im * b_re)


def tile_loss_value(object_patches, probe, measured_intensity):
    size = probe.shape[-1]
    table_re, table_im = dft_tables(size)
    kernel_re, kernel_im = fresnel_kernel(size)
    field_re, field_im = complex_times(
        probe[0], probe[1], object_patches[:, 0, 0], object_patches[:, 0, 1]
    )
    spec_re, spec_im = transform(field_re, field_im, table_re, table_im)
    spec_re, spec_im = complex_times(spec_re, spec_im, kernel_re, kernel_im)
    back_re, back_im = transform(spec_re, spec_im, table_re, -table_im)
    field_re, field_im = complex_times(
        back_re, back_im, object_patches[:, 1, 0], object_patches[:, 1, 1]
    )
    far_re, far_im = transform(field_re, field_im, table_re, table_im)
    model_amplitude = jnp.sqrt(far_re * far_re + far_im * far_im + 1.0)
    return 0.5 * jnp.sum((model_amplitude - measured_intensity) ** 2)


def body(object_planes, probe, positions, measured):
    tile_rows = object_planes.shape[2]
    tile_cols = object_planes.shape[3]
    slices = object_planes.shape[0]
    size = probe.shape[-1]
    offsets = positions[0, 0]
    measured_intensity = measured[0, 0]
    count_dev = offsets.shape[0]
    total_count = lax.axis_size("ty") * lax.axis_size("tx") * count_dev
    zero = jnp.zeros((), jnp.int32)
    for step in range(ITERS):
        right_tile = from_behind(object_planes, "tx", -1)
        below_tile = from_behind(object_planes, "ty", -1)
        corner_tile = from_behind(object_planes, ("ty", "tx"), -(lax.axis_size("tx") + 1))
        last_column = lax.axis_index("tx") == lax.axis_size("tx") - 1
        corner_tile = jnp.where(last_column, jnp.zeros_like(corner_tile), corner_tile)
        upper_pair = jnp.concatenate([object_planes, right_tile], axis=3)
        lower_pair = jnp.concatenate([below_tile, corner_tile], axis=3)
        extended = jnp.concatenate([upper_pair, lower_pair], axis=2)

        def cut_patch(offset):
            return lax.dynamic_slice(
                extended, (zero, zero, offset[0], offset[1]), (slices, 2, size, size)
            )

        object_patches = jax.vmap(cut_patch)(offsets)
        loss_value_total, backward_field = jax.vjp(
            lambda patch_argument, probe_argument: tile_loss_value(
                patch_argument, probe_argument, measured_intensity
            ),
            object_patches,
            probe,
        )
        grad_patches, probe_gradient = backward_field(jnp.ones_like(loss_value_total))

        def add_patch(index, grad_ext):
            offset = offsets[index]
            start = (zero, zero, offset[0], offset[1])
            old = lax.dynamic_slice(grad_ext, start, (slices, 2, size, size))
            return lax.dynamic_update_slice(grad_ext, old + grad_patches[index], start)

        grad_ext = lax.fori_loop(0, count_dev, add_patch, jnp.zeros_like(extended))
        arrived_cols = from_behind(grad_ext[:, :, :, tile_cols:], "tx", 1)
        column_sum = grad_ext[:, :, :, :tile_cols] + arrived_cols
        arrived_rows = from_behind(column_sum[:, :, tile_rows:], "ty", 1)
        grad_tile = column_sum[:, :, :tile_rows] + arrived_rows
        probe_sum = lax.psum(probe_gradient, ("ty", "tx"))
        object_planes = object_planes - 0.1 * grad_tile
        probe = probe - 0.5 / total_count * probe_sum
    return (object_planes, probe)


def solution(mesh):
    return jax.shard_map(
        body,
        mesh=mesh,
        in_specs=(
            P(None, None, "ty", "tx"),
            P(),
            P("ty", "tx", None, None),
            P("ty", "tx", None, None, None),
        ),
        out_specs=(P(None, None, "ty", "tx"), P()),
        check_vma=False,
    )
```

profile of v0, /device:TPU:1, one launch (start us, length us, event | category | flops | bytes accessed | tf_op | source)
XLA Modules:
  0.0 975.7 jit_solution(4255472306502076059)
XLA Ops:
  10.0 5.2 collective-permute-start.1
  18.2 7.9 collective-permute-done.2
  26.2 33.6 %collective-permute-done = f32[2,2,256,256]{3,2,1,0:T(8,128)} collective-permute-done((f32[2,2,256,256]{3,2,1,0:T(8,128)}, f32[2,2,256,256]{3,2,1,0:T(8,128)}, u32[]{:S(2)}, u32[]{:S(2)}) %collective-permute-start) | collective-permute-done | bytes 1048608 | tf_op jit(solution)/shard_map/ppermute | solution.py:14
  59.8 4.1 maximum_maximum_fusion
  64.1 8.0 while.30
  64.8 3.1 bitcast_dynamic-update-slice_fusion.4
  68.5 3.1 bitcast_dynamic-update-slice_fusion.4
  83.6 1.7 convolution_add_fusion.34
  95.3 1.8 convolution_add_fusion.32
  108.5 2.0 convolution_subtract_fusion.6
  112.1 1.9 fusion.133
  114.0 1.9 fusion.201
  115.8 1.9 fusion.29
  119.4 1.8 fusion.199
  121.3 1.9 fusion.28
  124.8 2.0 add_bitcast_fusion.7
  131.5 2.1 fusion.193
  143.4 1.8 fusion.21
  151.8 2.8 fusion.58
  156.1 2.5 broadcast.153.clone
  158.6 37.5 %while.28 = (s32[]{:T(128)}, f32[2,2,512,512]{3,2,1,0:T(8,128)}, s32[2,2]{1,0:T(2,128)S(1)}, f32[2,2,2,256,256]{4,3,0,2,1:T(8,128)}, s32[]{:T(128)}, /*index=5*/s32[]{:T(128)}, s32[]{:T(128)}) while((s32[]{:T(128)}, f32[2,2,512,512]{3,2,1,0:T(8,128)}, s32[2,2]{1,0:T(2,128)S(1)}, f32[2,2,2,256,256]{4,3,0,2,1:T(8,128)}, s32[]{:T(128)}, ...), condition=%wide.region_1.2_spmd, body=%wide.region_0.1_spmd.sunk | while | flops 262152 | bytes 5243077 | solution.py:109
  163.1 2.1 bitcast_add_fusion.4
  165.2 11.9 %dynamic_update_slice.16 = f32[2,2,512,512]{3,2,1,0:T(8,128)} dynamic-update-slice(f32[2,2,512,512]{3,2,1,0:T(8,128)} %get-tuple-element.413, f32[2,2,256,256]{3,2,1,0:T(8,128)S(1)} %bitcast_add_fusion.4, s32[]{:T(128)} %constant.109.clone.1..sunk, s32[]{:T(128)} %constant.109.clone.1..sunk, s32[]{:T(128)S(6)} %select_n.645, s32[]{:T(128)S(6)} %select_n.646) | dynamic-update-slice | bytes 2097156 | tf_op jit(solution)/shard_map/while/body/eval_jaxpr/dynamic_update_slice | solution.py:107
  181.6 2.1 bitcast_add_fusion.4
  183.8 12.2 %dynamic_update_slice.16 = f32[2,2,512,512]{3,2,1,0:T(8,128)} dynamic-update-slice(f32[2,2,512,512]{3,2,1,0:T(8,128)} %get-tuple-element.413, f32[2,2,256,256]{3,2,1,0:T(8,128)S(1)} %bitcast_add_fusion.4, s32[]{:T(128)} %constant.109.clone.1..sunk, s32[]{:T(128)} %constant.109.clone.1..sunk, s32[]{:T(128)S(6)} %select_n.645, s32[]{:T(128)S(6)} %select_n.646) | dynamic-update-slice | bytes 2097156 | tf_op jit(solution)/shard_map/while/body/eval_jaxpr/dynamic_update_slice | solution.py:107
  196.0 1.9 slice.109
  199.4 37.0 %collective-permute-done.3 = f32[2,2,512,256]{3,2,1,0:T(8,128)S(1)} collective-permute-done((f32[2,2,512,256]{3,2,1,0:T(8,128)S(1)}, f32[2,2,512,256]{3,2,1,0:T(8,128)S(1)}, u32[]{:S(2)}, u32[]{:S(2)}) %collective-permute-start.3) | collective-permute-done | bytes 2097184 | tf_op jit(solution)/shard_map/ppermute | solution.py:14
  236.9 2.1 collective-permute-start.4
  239.0 11.7 %collective-permute-done.4 = f32[2,2,256,256]{3,2,1,0:T(8,128)S(1)} collective-permute-done((f32[2,2,256,256]{3,2,1,0:T(8,128)S(1)}, f32[2,2,256,256]{3,2,1,0:T(8,128)S(1)}, u32[]{:S(2)}, u32[]{:S(2)}) %collective-permute-start.4) | collective-permute-done | bytes 1048608 | tf_op jit(solution)/shard_map/ppermute | solution.py:14
  253.8 1.9 collective-permute-start.6
  256.6 260.7 %all-reduce.15.cloned.1.call-done = f32[2,256,256]{2,1,0:T(8,128)} async-done(((f32[2,256,256]{2,1,0:T(8,128)}), f32[2,256,256]{2,1,0:T(8,128)}) %all-reduce.15.cloned.1.call-update) | async-done | bytes 524304 | tf_op jit(solution)/shard_map/psum | solution.py:114
  520.5 4.1 maximum_maximum_fusion.1
  524.8 8.0 while.31
  525.5 3.1 bitcast_dynamic-update-slice_fusion.5
  529.3 3.1 bitcast_dynamic-update-slice_fusion.5
  532.8 2.7 fusion.179
  535.5 2.6 fusion.183
  538.2 1.7 fusion.17
  543.0 1.7 fusion.16
  546.3 1.7 convolution_add_fusion.16
  558.0 1.8 convolution_add_fusion.14
  571.2 2.0 convolution_subtract_fusion
  574.7 1.9 fusion.111
  576.6 1.9 fusion.162
  578.5 1.9 fusion.11
  582.1 1.8 fusion.160
  583.9 1.9 fusion.10
  587.5 2.0 add_bitcast_fusion.3
  594.2 1.9 fusion.154
  605.9 1.9 fusion.3
  614.4 2.9 fusion.46
  618.8 2.5 broadcast.153
  621.2 37.5 %while.29 = (s32[]{:T(128)}, f32[2,2,512,512]{3,2,1,0:T(8,128)}, s32[2,2]{1,0:T(2,128)S(1)}, f32[2,2,2,256,256]{4,3,0,2,1:T(8,128)}, s32[]{:T(128)}, /*index=5*/s32[]{:T(128)}, s32[]{:T(128)}) while((s32[]{:T(128)}, f32[2,2,512,512]{3,2,1,0:T(8,128)}, s32[2,2]{1,0:T(2,128)S(1)}, f32[2,2,2,256,256]{4,3,0,2,1:T(8,128)}, s32[]{:T(128)}, ...), condition=%wide.region_8.9_spmd, body=%wide.region_7.8_spmd.sunk | while | flops 262152 | bytes 5243077 | solution.py:109
  625.8 2.1 bitcast_add_fusion.5
  627.9 11.9 %dynamic_update_slice.17 = f32[2,2,512,512]{3,2,1,0:T(8,128)} dynamic-update-slice(f32[2,2,512,512]{3,2,1,0:T(8,128)} %get-tuple-element.449, f32[2,2,256,256]{3,2,1,0:T(8,128)S(1)} %bitcast_add_fusion.5, s32[]{:T(128)} %constant.109.clone.1..sunk.1, s32[]{:T(128)} %constant.109.clone.1..sunk.1, s32[]{:T(128)S(6)} %select_n.647, s32[]{:T(128)S(6)} %select_n.648) | dynamic-update-slice | bytes 2097156 | tf_op jit(solution)/shard_map/while/body/eval_jaxpr/dynamic_update_slice | solution.py:107
  644.4 2.1 bitcast_add_fusion.5
  646.5 12.2 %dynamic_update_slice.17 = f32[2,2,512,512]{3,2,1,0:T(8,128)} dynamic-update-slice(f32[2,2,512,512]{3,2,1,0:T(8,128)} %get-tuple-element.449, f32[2,2,256,256]{3,2,1,0:T(8,128)S(1)} %bitcast_add_fusion.5, s32[]{:T(128)} %constant.109.clone.1..sunk.1, s32[]{:T(128)} %constant.109.clone.1..sunk.1, s32[]{:T(128)S(6)} %select_n.647, s32[]{:T(128)S(6)} %select_n.648) | dynamic-update-slice | bytes 2097156 | tf_op jit(solution)/shard_map/while/body/eval_jaxpr/dynamic_update_slice | solution.py:107
  658.7 1.9 slice.119
  660.6 2.8 collective-permute-start.8
  663.4 42.5 %collective-permute-done.8 = f32[2,2,512,256]{3,2,1,0:T(8,128)S(1)} collective-permute-done((f32[2,2,512,256]{3,2,1,0:T(8,128)S(1)}, f32[2,2,512,256]{3,2,1,0:T(8,128)S(1)}, u32[]{:S(2)}, u32[]{:S(2)}) %collective-permute-start.8) | collective-permute-done | bytes 2097184 | tf_op jit(solution)/shard_map/ppermute | solution.py:14
  706.5 6.3 collective-permute-start.9
  713.9 249.9 %all-reduce.17.cloned.1.call-done = f32[2,256,256]{2,1,0:T(8,128)} async-done(((f32[2,256,256]{2,1,0:T(8,128)}), f32[2,256,256]{2,1,0:T(8,128)}) %all-reduce.17.cloned.1.call-update) | async-done | bytes 524304 | tf_op jit(solution)/shard_map/psum | solution.py:114
  963.8 1.9 multiply_subtract_fusion
  965.7 2.7 fusion.37
  (161 shorter events, 135.3 us)
Async XLA Ops:
  7.2 52.6 %copy-start.6 = (f32[2,2,256,256]{3,2,1,0:T(8,128)S(1)}, f32[2,2,256,256]{3,2,1,0:T(8,128)}, u32[]{:S(2)}) copy-start(f32[2,2,256,256]{3,2,1,0:T(8,128)} %param.8) | copy-start | bytes 3145732
  7.2 510.1 %all-reduce.15.cloned.1.call-start = ((), (), s32[]{:S(2)}) async-start(), calls=%async_computation | async-start | bytes 1048576 | tf_op jit(solution)/shard_map/psum | solution.py:114
  7.2 18.9 %collective-permute-start.2 = (f32[2,2,256,256]{3,2,1,0:T(8,128)}, f32[2,2,256,256]{3,2,1,0:T(8,128)S(1)}, u32[]{:S(2)}, u32[]{:S(2)}) collective-permute-start(f32[2,2,256,256]{3,2,1,0:T(8,128)} %param.8), channel_id=1, source_target_pairs={{17,0},{18,1},{19,2},{20,3},{21,4},{22,5},{23,6},{24,7},{25,8},{26... | collective-permute-start | bytes 3145736 | tf_op jit(solution)/shard_map/ppermute | solution.py:14
  8.7 51.1 %collective-permute-start = (f32[2,2,256,256]{3,2,1,0:T(8,128)}, f32[2,2,256,256]{3,2,1,0:T(8,128)}, u32[]{:S(2)}, u32[]{:S(2)}) collective-permute-start(f32[2,2,256,256]{3,2,1,0:T(8,128)} %param.8), channel_id=1, source_target_pairs={{1,0},{2,1},{3,2},{4,3},{5,4},{6,5},{7,6},{8,7},{9,8},{10,9},{11,1... | collective-permute-start | bytes 3145736 | tf_op jit(solution)/shard_map/ppermute | solution.py:14
  10.0 49.9 %collective-permute-start.1 = (f32[2,2,256,256]{3,2,1,0:T(8,128)}, f32[2,2,256,256]{3,2,1,0:T(8,128)}, u32[]{:S(2)}, u32[]{:S(2)}) collective-permute-start(f32[2,2,256,256]{3,2,1,0:T(8,128)} %param.8), channel_id=1, source_target_pairs={{16,0},{32,16},{48,32},{64,48},{80,64},{96,80},{112,96},{128,112},... | collective-permute-start | bytes 3145736 | tf_op jit(solution)/shard_map/ppermute | solution.py:14
  106.9 5.2 copy-start.17
  156.1 2.5 copy-start.16
  196.0 40.4 %copy-start.1 = (f32[2,2,512,512]{3,2,1,0:T(8,128)S(1)}, f32[2,2,512,512]{3,2,1,0:T(8,128)}, u32[]{:S(2)}) copy-start(f32[2,2,512,512]{3,2,1,0:T(8,128)} %get-tuple-element.160) | copy-start | bytes 12582916
  197.9 38.5 %collective-permute-start.3 = (f32[2,2,512,256]{3,2,1,0:T(8,128)S(1)}, f32[2,2,512,256]{3,2,1,0:T(8,128)S(1)}, u32[]{:S(2)}, u32[]{:S(2)}) collective-permute-start(f32[2,2,512,256]{3,2,1,0:T(8,128)S(1)} %slice.109), channel_id=1, source_target_pairs={{0,1},{1,2},{2,3},{3,4},{4,5},{5,6},{6,7},{7,8},{8,9},{9,10},{10,1... | collective-permute-start | bytes 6291464 | tf_op jit(solution)/shard_map/ppermute | solution.py:14
  236.8 13.9 %copy-start.7 = (f32[2,2,256,256]{3,2,1,0:T(8,128)S(1)}, f32[2,2,256,256]{3,2,1,0:T(8,128)}, u32[]{:S(2)}) copy-start(f32[2,2,256,256]{3,2,1,0:T(8,128)} %param.8) | copy-start | bytes 3145732
  236.9 15.5 %copy-start.13 = (f32[256,256]{1,0:T(8,128)S(1)}, f32[256,256]{1,0:T(8,128)}, u32[]{:S(2)}) copy-start(f32[256,256]{1,0:T(8,128)} %get-tuple-element.191) | copy-start | bytes 786436
  236.9 15.5 %copy-start.14 = (f32[256,256]{1,0:T(8,128)S(1)}, f32[256,256]{1,0:T(8,128)}, u32[]{:S(2)}) copy-start(f32[256,256]{1,0:T(8,128)} %get-tuple-element.196) | copy-start | bytes 786436
  236.9 15.5 %copy-start.15 = (f32[256,256]{1,0:T(8,128)S(1)}, f32[256,256]{1,0:T(8,128)}, u32[]{:S(2)}) copy-start(f32[256,256]{1,0:T(8,128)} %get-tuple-element.197) | copy-start | bytes 786436
  236.9 13.8 %collective-permute-start.4 = (f32[2,2,256,256]{3,2,1,0:T(8,128)S(1)}, f32[2,2,256,256]{3,2,1,0:T(8,128)S(1)}, u32[]{:S(2)}, u32[]{:S(2)}) collective-permute-start(f32[2,2,256,256]{3,2,1,0:T(8,128)S(1)} %slice.161), channel_id=1, source_target_pairs={{0,16},{16,32},{32,48},{48,64},{64,80},{80,96},{96,112},{112,128},... | collective-permute-start | bytes 3145736 | tf_op jit(solution)/shard_map/ppermute | solution.py:14
  250.9 269.6 %copy-start.2 = (f32[2,2,256,256]{3,2,1,0:T(8,128)}, f32[2,2,256,256]{3,2,1,0:T(8,128)S(1)}, u32[]{:S(2)}) copy-start(f32[2,2,256,256]{3,2,1,0:T(8,128)S(1)} %fusion.39) | copy-start | bytes 3145732
  250.9 266.4 %copy-start.8 = (f32[2,256,256]{2,1,0:T(8,128)S(1)}, f32[2,256,256]{2,1,0:T(8,128)}, u32[]{:S(2)}) copy-start(f32[2,256,256]{2,1,0:T(8,128)} %param.9) | copy-start | bytes 1572868
  250.9 268.2 %collective-permute-start.7 = (f32[2,2,256,256]{3,2,1,0:T(8,128)S(1)}, f32[2,2,256,256]{3,2,1,0:T(8,128)}, u32[]{:S(2)}, u32[]{:S(2)}) collective-permute-start(f32[2,2,256,256]{3,2,1,0:T(8,128)S(1)} %fusion.39), channel_id=1, source_target_pairs={{17,0},{18,1},{19,2},{20,3},{21,4},{22,5},{23,6},{24,7},{25,8},{26... | collective-permute-start | bytes 3145736 | tf_op jit(solution)/shard_map/ppermute | solution.py:14
  252.5 268.0 %collective-permute-start.5 = (f32[2,2,256,256]{3,2,1,0:T(8,128)S(1)}, f32[2,2,256,256]{3,2,1,0:T(8,128)}, u32[]{:S(2)}, u32[]{:S(2)}) collective-permute-start(f32[2,2,256,256]{3,2,1,0:T(8,128)S(1)} %fusion.39), channel_id=1, source_target_pairs={{1,0},{2,1},{3,2},{4,3},{5,4},{6,5},{7,6},{8,7},{9,8},{10,9},{11,1... | collective-permute-start | bytes 3145736 | tf_op jit(solution)/shard_map/ppermute | solution.py:14
  253.8 266.7 %collective-permute-start.6 = (f32[2,2,256,256]{3,2,1,0:T(8,128)S(1)}, f32[2,2,256,256]{3,2,1,0:T(8,128)}, u32[]{:S(2)}, u32[]{:S(2)}) collective-permute-start(f32[2,2,256,256]{3,2,1,0:T(8,128)S(1)} %fusion.39), channel_id=1, source_target_pairs={{16,0},{32,16},{48,32},{64,48},{80,64},{96,80},{112,96},{128,112},... | collective-permute-start | bytes 3145736 | tf_op jit(solution)/shard_map/ppermute | solution.py:14
  256.6 707.2 %all-reduce.17.cloned.1.call-start = ((), (), s32[]{:S(2)}) async-start(), calls=%async_computation.1 | async-start | bytes 1048576 | tf_op jit(solution)/shard_map/psum | solution.py:114
  532.8 5.4 copy-start.5
  569.5 5.2 copy-start.18
  658.7 47.2 %copy-start = (f32[2,2,512,512]{3,2,1,0:T(8,128)S(1)}, f32[2,2,512,512]{3,2,1,0:T(8,128)}, u32[]{:S(2)}) copy-start(f32[2,2,512,512]{3,2,1,0:T(8,128)} %get-tuple-element.161) | copy-start | bytes 12582916
  660.6 45.4 %collective-permute-start.8 = (f32[2,2,512,256]{3,2,1,0:T(8,128)S(1)}, f32[2,2,512,256]{3,2,1,0:T(8,128)S(1)}, u32[]{:S(2)}, u32[]{:S(2)}) collective-permute-start(f32[2,2,512,256]{3,2,1,0:T(8,128)S(1)} %slice.119), channel_id=1, source_target_pairs={{0,1},{1,2},{2,3},{3,4},{4,5},{5,6},{6,7},{7,8},{8,9},{9,10},{10,1... | collective-permute-start | bytes 6291464 | tf_op jit(solution)/shard_map/ppermute | solution.py:14
  706.4 6.5 copy-start.4
  706.4 6.5 copy-start.11
  706.4 6.5 copy-start.12
  706.4 6.5 copy-start.9
  706.4 6.5 copy-start.10
  706.5 259.1 %collective-permute-start.9 = (f32[2,2,256,256]{3,2,1,0:T(8,128)S(1)}, f32[2,2,256,256]{3,2,1,0:T(8,128)}, u32[]{:S(2)}, u32[]{:S(2)}) collective-permute-start(f32[2,2,256,256]{3,2,1,0:T(8,128)S(1)} %slice.165), channel_id=1, source_target_pairs={{0,16},{16,32},{32,48},{48,64},{64,80},{80,96},{96,112},{112,128},... | collective-permute-start | bytes 3145736 | tf_op jit(solution)/shard_map/ppermute | solution.py:14
  712.9 252.7 %copy-start.3 = (f32[2,2,256,256]{3,2,1,0:T(8,128)S(1)}, f32[2,2,256,256]{3,2,1,0:T(8,128)}, u32[]{:S(2)}) copy-start(f32[2,2,256,256]{3,2,1,0:T(8,128)} %copy-done.2) | copy-start | bytes 3145732
Sparse Core Ops, SparseCore 0:
  256.7 260.5 all-reduce.14
  714.0 249.7 all-reduce.16
where the time goes:
time: 982 us; the launch traced here: 976 us
  waiting for transfers between devices  643 us (65%)
  matrix products  166 us (17%)
  local copies, waits for them, and re-layouts  77.2 us (8%)
  other arithmetic  31.6 us (3%)
  starting transfers between devices  25.2 us (3%)
  loops' own time  16.5 us (2%)
  between operations  15.7 us (2%)
    psum x2, waiting for transfers between devices, body(): probe_sum = lax.psum(probe_gradient, ('ty', 'tx'))  511 us
    dot_general x96, matrix products, exact_product(): jnp.matmul(left, right, precision=lax.Precision.HIGHEST, preferred_elemen...  166 us
    ppermute x10, waiting for transfers between devices, from_behind(): return lax.ppermute(shard, axis, pairs)  133 us
    dynamic_update_slice x4, local copies, waits for them, and re-layouts, add_patch(): return lax.dynamic_update_slice(grad_ext, old + grad_patches[index], start)  48.4 us
    ppermute x10, starting transfers between devices, from_behind(): return lax.ppermute(shard, axis, pairs)  25.1 us
  transfers between devices with their start and end apart: 12, of which 7 were waited for; matrix products, arithmetic and copies ran while one was open for 1% of the time, Pallas kernels for 0%

commit v1 on v0

v1 whole, which is shorter than its diff:
```python
import math

import jax
import jax.numpy as jnp
import numpy as np
from jax import lax
from jax.experimental import pallas as pl
from jax.experimental.pallas import tpu as pltpu
from jax.sharding import PartitionSpec as P
import ml_dtypes

MESH = pl.DeviceIdType.MESH
F32 = jnp.float32
BF16 = jnp.bfloat16
N = 256
H = 128
ITERS = 2
RB = 16
CHUNKS = [(s, p, h * H, H) for s in (1, 0) for p in (0, 1) for h in (0, 1)]
NCH = len(CHUNKS)
OBJ_STEP = 0.1


def real_form(block):
    top = np.concatenate([block.real, -block.imag], axis=1)
    low = np.concatenate([block.imag, block.real], axis=1)
    return np.concatenate([top, low], axis=0)


def tables():
    k = np.arange(N)
    dft = np.exp(-2j * math.pi * ((k[:, None] * k[None, :]) % N) / N) / math.sqrt(N)
    chirp = np.exp(1j * math.pi * ((k * k) % (2 * N)) / N)
    prop = np.exp(-0.25j * math.pi) * chirp[:, None] * dft * chirp[None, :]
    kinds = []
    for kind in range(4):
        pars = []
        for par in (0, 1):
            if kind < 2:
                mat = real_form(prop[par::2, :H])
            else:
                mat = real_form(dft[:H, par::2])
            if kind % 2:
                mat = mat.T
            mat = mat.astype(np.float32)
            hi = mat.astype(ml_dtypes.bfloat16)
            lo = (mat - hi.astype(np.float32)).astype(ml_dtypes.bfloat16)
            pars.append(np.stack([hi, lo]))
        kinds.append(np.stack(pars))
    return np.stack(kinds)


def shuffles():
    perm = np.zeros((N, N), np.float32)
    j = np.arange(H)
    perm[j, 2 * j] = 1
    perm[H + j, 2 * j + 1] = 1
    return np.stack([perm, perm.T]).astype(ml_dtypes.bfloat16)


def split(x):
    hi = x.astype(BF16)
    return hi, (x - hi.astype(F32)).astype(BF16)


def split3(x):
    hi = x.astype(BF16)
    rest = x - hi.astype(F32)
    mid = rest.astype(BF16)
    return hi, mid, (rest - mid.astype(F32)).astype(BF16)


def dot(a, b):
    return jnp.dot(a, b, preferred_element_type=F32)


def permute_rows(perm, x):
    hi, mid, lo = split3(x)
    return dot(perm, hi) + dot(perm, mid) + dot(perm, lo)


def permute_cols(perm, x):
    hi, mid, lo = split3(x)
    return dot(hi, perm) + dot(mid, perm) + dot(lo, perm)


def blocks(count, body):
    def step(b, carry):
        body(pl.multiple_of(b * RB, RB))
        return carry

    lax.fori_loop(0, count, step, 0)


def make_kernel(n_ty, n_tx):
    ny = 4 if n_tx == 16 else 2
    nx = n_tx // ny
    nz = n_ty // 2
    xr = N // nx
    yr = xr // ny

    def kernel(pos, obj, probe_in, meas_in, mats_in, perm_in, obj_out, probe_out,
               tor, tbc1, tbc2, gor, gbc, ra, rb, rc, t0, t1, pw, gp, gsum, probe,
               dhi, dlo, lhi, llo, gbuf, rbuf, psi, meas, mats, perm, stage, result,
               r0, r1, r2, rz, send, recv, local):
        ty = lax.axis_index("ty")
        tx = lax.axis_index("tx")
        up = (lax.rem(ty + n_ty - 1, n_ty), tx)
        down = (lax.rem(ty + 1, n_ty), tx)
        left = (ty, lax.rem(tx + n_tx - 1, n_tx))
        right = (ty, lax.rem(tx + 1, n_tx))
        core = lax.rem(ty, 2)
        z = lax.div(ty, 2)
        x = lax.div(tx, ny)
        y = lax.rem(tx, ny)
        mate = (ty + 1 - 2 * core, tx)
        xs = [(ty, lax.rem(x + d, nx) * ny + y) for d in range(1, nx)]
        ys = [(ty, x * ny + lax.rem(y + d, ny)) for d in range(1, ny)]
        zs = [(lax.rem(z + d, nz) * 2 + core, tx) for d in range(1, nz)]
        has_above = jnp.where(ty > 0, 1.0, 0.0).astype(F32)
        has_below = jnp.where(ty < n_ty - 1, 1.0, 0.0).astype(F32)
        has_left = jnp.where(tx > 0, 1.0, 0.0).astype(F32)
        has_right = jnp.where(tx < n_tx - 1, 1.0, 0.0).astype(F32)

        used = [0]

        def remote(src, dst, device):
            index = used[0]
            used[0] += 1
            return pltpu.make_async_remote_copy(
                src_ref=src, dst_ref=dst, send_sem=send.at[index], recv_sem=recv.at[index],
                device_id=device, device_id_type=MESH)

        def rows_of(chunk):
            s, p, r, n = chunk
            return s, p, pl.ds(r, n)

        loads = [
            pltpu.make_async_copy(obj.at[1], stage, local.at[0]),
            pltpu.make_async_copy(perm_in, perm, local.at[1]),
            pltpu.make_async_copy(obj.at[0], tor.at[0, 0], local.at[2]),
            pltpu.make_async_copy(probe_in, probe.at[0], local.at[3]),
            pltpu.make_async_copy(mats_in, mats, local.at[4]),
            pltpu.make_async_copy(meas_in, meas, local.at[5]),
        ]
        for copy in loads:
            copy.start()

        barrier = pltpu.get_barrier_semaphore()
        partners = [left, right, up, down] + xs + ys + zs
        for device in partners:
            pl.semaphore_signal(barrier, inc=1, device_id=device, device_id_type=MESH)
        pl.semaphore_wait(barrier, len(partners))

        first_chunks = CHUNKS[NCH // 2:] + CHUNKS[:NCH // 2]
        own_left, own_up, right_up = [], [], []
        for chunk in first_chunks:
            s, p, rows = rows_of(chunk)
            src = obj.at[0, p, rows] if s == 0 else tor.at[0, 1, p, rows]
            own_left.append(remote(src, tor.at[1, s, p, rows], left))
            own_up.append(remote(src, tbc1.at[0, s, p, rows], up))
            right_up.append(remote(tor.at[1, s, p, rows], tbc1.at[1, s, p, rows], up))
        for i in range(NCH // 2):
            own_left[i].start()
            own_up[i].start()
        loads[0].wait()
        loads[1].wait()
        for p in (0, 1):
            tor[0, 1, p] = permute_cols(perm[1], permute_rows(perm[0], stage[p]))
            for i in range(NCH // 2 + p * NCH // 4, NCH // 2 + (p + 1) * NCH // 4):
                own_left[i].start()
                own_up[i].start()

        row_in_block = lax.broadcasted_iota(jnp.int32, (RB, N), 0)
        col_index = lax.broadcasted_iota(jnp.int32, (RB, N), 1)
        col_half = lax.broadcasted_iota(jnp.int32, (RB, H), 1)
        row_half = lax.broadcasted_iota(jnp.int32, (RB, H), 0)
        row_sign = jnp.where(lax.rem(row_in_block, 2) == 1, -1.0, 1.0).astype(F32)
        col_sign = jnp.where(lax.rem(col_half, 2) == 1, -1.0, 1.0).astype(F32)
        offsets = [(pos[0], pos[1]), (pos[2], pos[3])]

        def window(tbc, s, p, rows, cols, row_ok, col_ok):
            upper = jnp.where(col_ok, tor[0, s, p, rows, cols], has_right * tor[1, s, p, rows, cols])
            lower = jnp.where(col_ok, tbc[0, s, p, rows, cols], has_right * tbc[1, s, p, rows, cols])
            return jnp.where(row_ok, upper, has_below * lower)

        def put_d(par, rr, k, cols, value):
            hi, lo = split(value)
            rows = pl.ds(rr + k * H, RB)
            dhi[par, rows, cols] = hi
            dlo[par, rows, cols] = lo

        def put_l(cp, rows, k, value):
            hi, lo = split(value)
            cols = pl.ds(k * H, H)
            lhi[cp, rows, cols] = hi
            llo[cp, rows, cols] = lo

        def left_product(kind):
            for par in (0, 1):
                a_hi, a_lo = mats[kind, par, 0], mats[kind, par, 1]
                gbuf[par] = dot(a_lo, dhi[par]) + dot(a_hi, dlo[par]) + dot(a_hi, dhi[par])

        def right_product(kind, out):
            for cp in (0, 1):
                b_hi, b_lo = mats[kind, cp, 0], mats[kind, cp, 1]
                out[cp] = dot(lhi[cp], b_lo) + dot(llo[cp], b_hi) + dot(lhi[cp], b_hi)

        def col_split(signed):
            def body(rr):
                for par in (0, 1):
                    for q in (0, 1):
                        for k in (0, 1):
                            low = gbuf[par, pl.ds(rr + k * H, RB), pl.ds(q * N, H)]
                            high = gbuf[par, pl.ds(rr + k * H, RB), pl.ds(q * N + H, H)]
                            if signed:
                                high = high * col_sign
                            rows = pl.ds(rr + q * N + par * H, RB)
                            put_l(0, rows, k, low + high)
                            put_l(1, rows, k, low - high)
            blocks(H // RB, body)

        def col_join(signed):
            def body(rr):
                for par in (0, 1):
                    for q in (0, 1):
                        rows = pl.ds(rr + q * N + par * H, RB)
                        for k in (0, 1):
                            even = rbuf[0, rows, pl.ds(k * H, H)]
                            odd = rbuf[1, rows, pl.ds(k * H, H)]
                            high = even - odd
                            if signed:
                                high = high * col_sign
                            put_d(par, rr, k, pl.ds(q * N, H), even + odd)
                            put_d(par, rr, k, pl.ds(q * N + H, H), high)
            blocks(H // RB, body)

        def roll_probe(step):
            for q in (0, 1):
                for k in (0, 1):
                    moved = pltpu.roll(probe[step, k], offsets[q][0], 0)
                    pw[q, k] = pltpu.roll(moved, offsets[q][1], 1)

        def forward_first(tbc):
            def body(rr):
                for q in (0, 1):
                    r, c = offsets[q]
                    col_ok = col_index >= c
                    fields = []
                    for half in (0, 1):
                        rows = pl.ds(rr + half * H, RB)
                        row_ok = row_in_block + (rr + half * H) >= r
                        tr = window(tbc, 0, 0, rows, slice(None), row_ok, col_ok)
                        ti = window(tbc, 0, 1, rows, slice(None), row_ok, col_ok)
                        t0[q, 0, rows] = tr
                        t0[q, 1, rows] = ti
                        pr, pi = pw[q, 0, rows], pw[q, 1, rows]
                        fields.append((pr * tr - pi * ti, pr * ti + pi * tr))
                    for k in (0, 1):
                        high = fields[1][k] * row_sign
                        put_d(0, rr, k, pl.ds(q * N, N), fields[0][k] + high)
                        put_d(1, rr, k, pl.ds(q * N, N), fields[0][k] - high)
            blocks(H // RB, body)
            left_product(0)
            col_split(True)
            right_product(1, psi)

        def forward_rest(tbc):
            def body(rr):
                for q in (0, 1):
                    r, c = offsets[q]
                    for par in (0, 1):
                        trows = pl.ds(rr + par * H, RB)
                        rows = pl.ds(rr + q * N + par * H, RB)
                        row_ok = 2 * (row_half + rr) + par >= r
                        for cp in (0, 1):
                            col_ok = 2 * col_half + cp >= c
                            cols = pl.ds(cp * H, H)
                            tr = window(tbc, 1, 0, trows, cols, row_ok, col_ok)
                            ti = window(tbc, 1, 1, trows, cols, row_ok, col_ok)
                            t1[q, 0, trows, cols] = tr
                            t1[q, 1, trows, cols] = ti
                            fr = psi[cp, rows, pl.ds(0, H)]
                            fi = psi[cp, rows, pl.ds(H, H)]
                            put_l(cp, rows, 0, fr * tr - fi * ti)
                            put_l(cp, rows, 1, fr * ti + fi * tr)
            blocks(H // RB, body)
            right_product(3, rbuf)
            col_join(False)
            left_product(2)

        def backward_first():
            def body(rr):
                for q in (0, 1):
                    cols = pl.ds(q * N, N)
                    er, ei = gbuf[0, pl.ds(rr, RB), cols], gbuf[0, pl.ds(rr + H, RB), cols]
                    odr, odi = gbuf[1, pl.ds(rr, RB), cols], gbuf[1, pl.ds(rr + H, RB), cols]
                    halves = []
                    for half, (fr, fi) in enumerate(((er + odr, ei + odi), (er - odr, ei - odi))):
                        m = meas[q, pl.ds(rr + half * H, RB)]
                        weight = 1.0 - m * lax.rsqrt(fr * fr + fi * fi + 1.0)
                        halves.append((weight * fr, weight * fi))
                    for k in (0, 1):
                        put_d(0, rr, k, cols, halves[0][k] + halves[1][k])
                        put_d(1, rr, k, cols, halves[0][k] - halves[1][k])
            blocks(H // RB, body)
            left_product(3)
            col_split(False)
            right_product(2, rbuf)

        def scatter(s, p, rows, cols, values, row_oks, col_oks):
            zero = jnp.zeros_like(values[0])
            upper = [jnp.where(row_oks[q], values[q], zero) for q in (0, 1)]
            lower = [values[q] - upper[q] for q in (0, 1)]
            for part, dst in ((upper, gor), (lower, gbc)):
                kept = [jnp.where(col_oks[q], part[q], zero) for q in (0, 1)]
                dst[0, s, p, rows, cols] = kept[0] + kept[1]
                dst[1, s, p, rows, cols] = (part[0] - kept[0]) + (part[1] - kept[1])

        def backward_second():
            def body(rr):
                for par in (0, 1):
                    trows = pl.ds(rr + par * H, RB)
                    row_oks = [2 * (row_half + rr) + par >= offsets[q][0] for q in (0, 1)]
                    for cp in (0, 1):
                        col_oks = [2 * col_half + cp >= offsets[q][1] for q in (0, 1)]
                        cols = pl.ds(cp * H, H)
                        grads = []
                        for q in (0, 1):
                            rows = pl.ds(rr + q * N + par * H, RB)
                            gr, gi = rbuf[cp, rows, pl.ds(0, H)], rbuf[cp, rows, pl.ds(H, H)]
                            fr, fi = psi[cp, rows, pl.ds(0, H)], psi[cp, rows, pl.ds(H, H)]
                            tr, ti = t1[q, 0, trows, cols], t1[q, 1, trows, cols]
                            grads.append((gr * fr + gi * fi, gi * fr - gr * fi))
                            put_l(cp, rows, 0, gr * tr + gi * ti)
                            put_l(cp, rows, 1, gi * tr - gr * ti)
                        for k in (0, 1):
                            scatter(1, k, trows, cols, [g[k] for g in grads], row_oks, col_oks)
            blocks(H // RB, body)

        def backward_last():
            right_product(0, rbuf)
            col_join(True)
            left_product(1)

            def body(rr):
                col_oks = [col_index >= offsets[q][1] for q in (0, 1)]
                for half in (0, 1):
                    rows = pl.ds(rr + half * H, RB)
                    row_oks = [row_in_block + (rr + half * H) >= offsets[q][0] for q in (0, 1)]
                    grads = []
                    for q in (0, 1):
                        cols = pl.ds(q * N, N)
                        er, ei = gbuf[0, pl.ds(rr, RB), cols], gbuf[0, pl.ds(rr + H, RB), cols]
                        odr, odi = gbuf[1, pl.ds(rr, RB), cols], gbuf[1, pl.ds(rr + H, RB), cols]
                        if half:
                            ur, ui = (er - odr) * row_sign, (ei - odi) * row_sign
                        else:
                            ur, ui = er + odr, ei + odi
                        pr, pi = pw[q, 0, rows], pw[q, 1, rows]
                        tr, ti = t0[q, 0, rows], t0[q, 1, rows]
                        grads.append((ur * pr + ui * pi, ui * pr - ur * pi))
                        gp[q, 0, rows] = ur * tr + ui * ti
                        gp[q, 1, rows] = ui * tr - ur * ti
                    for k in (0, 1):
                        scatter(0, k, rows, slice(None), [g[k] for g in grads], row_oks, col_oks)
            blocks(H // RB, body)

        def sum_probe():
            for k in (0, 1):
                parts = []
                for q in (0, 1):
                    back = pltpu.roll(gp[q, k], lax.rem(N - offsets[q][0], N), 0)
                    parts.append(pltpu.roll(back, lax.rem(N - offsets[q][1], N), 1))
                gsum[k] = parts[0] + parts[1]

        def reduction(step):
            buf = step
            c0 = remote(gsum.at[1 - core], r0.at[buf], mate)
            c1 = [remote(r0.at[buf, pl.ds(pl.multiple_of(lax.rem(x + d, nx) * xr, xr), xr)],
                         r1.at[buf, d - 1], xs[d - 1]) for d in range(1, nx)]
            c2 = [remote(r1.at[buf, nx - 1, pl.ds(pl.multiple_of(lax.rem(y + d, ny) * yr, yr), yr)],
                         r2.at[buf, d - 1], ys[d - 1]) for d in range(1, ny)]
            c3 = [remote(rz.at[buf, z], rz.at[buf, z], zs[d - 1]) for d in range(1, nz)]
            base_x = pl.multiple_of(x * xr, xr)
            base_y = pl.multiple_of(y * yr, yr)
            base = pl.multiple_of(x * xr + y * yr, yr)
            mine = probe.at[step + 1, core, pl.ds(base, yr)]
            strip = probe.at[step + 1, core, pl.ds(base_x, xr)]
            plane = probe.at[step + 1, core]
            c4 = [remote(mine, mine, ys[d - 1]) for d in range(1, ny)]
            c5 = [remote(strip, strip, xs[d - 1]) for d in range(1, nx)]
            c6 = remote(plane, plane, mate)

            def a0():
                c0.start()

            def a1():
                c0.wait_recv()
                r0[buf] = r0[buf] + gsum[core]
                for c in c1:
                    c.start()

            def a2():
                total = r0[buf, pl.ds(base_x, xr)]
                for i, c in enumerate(c1):
                    c.wait_recv()
                    total = total + r1[buf, i]
                r1[buf, nx - 1] = total
                for c in c2:
                    c.start()

            def a3():
                total = r1[buf, nx - 1, pl.ds(base_y, yr)]
                for i, c in enumerate(c2):
                    c.wait_recv()
                    total = total + r2[buf, i]
                rz[buf, z] = total
                for c in c3:
                    c.start()

            def a4():
                for c in c3:
                    c.wait_recv()
                total = rz[buf, 0]
                for i in range(1, nz):
                    total = total + rz[buf, i]
                scale = 0.5 / (n_ty * n_tx * 2)
                probe[step + 1, core, pl.ds(base, yr)] = probe[step, core, pl.ds(base, yr)] - scale * total
                for c in c4:
                    c.start()

            def a5():
                for c in c4:
                    c.wait_recv()
                for c in c5:
                    c.start()

            def a6():
                for c in c5:
                    c.wait_recv()
                c6.start()

            def a7():
                c6.wait_recv()
                for c in [c0, c6] + c1 + c2 + c3 + c4 + c5:
                    c.wait_send()

            return [a0, a1, a2, a3, a4, a5, a6, a7]

        def grads_down(step):
            return [remote(gbc.at[:, s, p, rows], ra.at[step, :, s, p, rows], down)
                    for s, p, rows in map(rows_of, CHUNKS)]

        half = NCH // 2
        for i in range(half):
            own_left[i].wait_recv()
            right_up[i].start()
        loads[2].wait()
        loads[3].wait()
        roll_probe(0)
        own_left[half].wait_recv()
        right_up[half].start()
        for i in range(half):
            own_up[i].wait_recv()
            right_up[i].wait_recv()
        loads[4].wait()
        forward_first(tbc1)
        for i in range(half + 1, NCH):
            own_left[i].wait_recv()
            right_up[i].start()
        for i in range(half, NCH):
            own_up[i].wait_recv()
            right_up[i].wait_recv()
        loads[5].wait()
        forward_rest(tbc1)
        backward_first()
        backward_second()
        for c in own_left + own_up + right_up:
            c.wait_send()

        a_sends = grads_down(0)
        b_right, b_left, c_up = [], [], []
        for s, p, rows in map(rows_of, CHUNKS):
            b_right.append(remote(gor.at[1, s, p, rows], rb.at[0, s, p, rows], right))
            b_left.append(remote(gor.at[0, s, p, rows], rc.at[s, p, rows], left))
            c_up.append(remote(tor.at[:, s, p, rows], tbc2.at[:, s, p, rows], up))
        for i in range(half):
            a_sends[i].start()
        backward_last()
        for i in range(half, NCH):
            a_sends[i].start()
        sum_probe()
        actions = reduction(0)
        actions.pop(0)()

        def add_above(i, step):
            s, p, rows = rows_of(CHUNKS[i])
            a_sends[i].wait_recv()
            for part in (0, 1):
                gor[part, s, p, rows] = gor[part, s, p, rows] + has_above * ra[step, part, s, p, rows]

        def mid_b(i):
            add_above(i, 0)
            b_right[i].start()
            b_left[i].start()

        def mid_c(i):
            s, p, rows = rows_of(CHUNKS[i])
            b_right[i].wait_recv()
            b_left[i].wait_recv()
            tor[0, s, p, rows] = tor[0, s, p, rows] - OBJ_STEP * (
                gor[0, s, p, rows] + has_left * rb[0, s, p, rows])
            tor[1, s, p, rows] = tor[1, s, p, rows] - OBJ_STEP * (
                gor[1, s, p, rows] + has_right * rc[s, p, rows])
            c_up[i].start()

        mid_b(0)
        for i in range(1, NCH):
            mid_b(i)
            mid_c(i - 1)
            if actions:
                actions.pop(0)()
        mid_c(NCH - 1)
        while actions:
            actions.pop(0)()
        roll_probe(1)
        for c in c_up:
            c.wait_recv()
        for c in a_sends + b_right + b_left:
            c.wait_send()

        forward_first(tbc2)
        forward_rest(tbc2)
        backward_first()
        backward_second()
        for c in c_up:
            c.wait_send()
        a_sends = grads_down(1)
        b_right = [remote(gor.at[1, s, p, rows], rb.at[1, s, p, rows], right)
                   for s, p, rows in map(rows_of, CHUNKS)]
        for i in range(half):
            a_sends[i].start()
        backward_last()
        for i in range(half, NCH):
            a_sends[i].start()
        sum_probe()
        actions = reduction(1)
        actions.pop(0)()

        def end_b(i):
            add_above(i, 1)
            b_right[i].start()

        def end_c(i):
            s, p, rows = rows_of(CHUNKS[i])
            b_right[i].wait_recv()
            value = tor[0, s, p, rows] - OBJ_STEP * (gor[0, s, p, rows] + has_left * rb[1, s, p, rows])
            if s == 0:
                result[0, p, rows] = value
            else:
                stage[p, rows] = value

        stores = []
        end_b(0)
        for i in range(1, NCH):
            end_b(i)
            end_c(i - 1)
            if actions:
                actions.pop(0)()
            if i == half + 1:
                for p in (0, 1):
                    result[1, p] = permute_cols(perm[0], permute_rows(perm[1], stage[p]))
                stores.append(pltpu.make_async_copy(result.at[1], obj_out.at[1], local.at[6]))
                stores[-1].start()
        end_c(NCH - 1)
        stores.append(pltpu.make_async_copy(result.at[0], obj_out.at[0], local.at[7]))
        stores[-1].start()
        while actions:
            actions.pop(0)()
        stores.append(pltpu.make_async_copy(probe.at[2], probe_out, local.at[8]))
        stores[-1].start()
        for c in a_sends + b_right:
            c.wait_send()
        for copy in stores:
            copy.wait()

    copies = 3 * NCH + 4 * NCH + 2 * NCH + 2 * (2 + 2 * (nx - 1) + 2 * (ny - 1) + nz - 1)
    field = (2, 2, N, N)
    scratch = dict(
        tor=pltpu.VMEM((2,) + field, F32),
        tbc1=pltpu.VMEM((2,) + field, F32),
        tbc2=pltpu.VMEM((2,) + field, F32),
        gor=pltpu.VMEM((2,) + field, F32),
        gbc=pltpu.VMEM((2,) + field, F32),
        ra=pltpu.VMEM((2, 2) + field, F32),
        rb=pltpu.VMEM((2,) + field, F32),
        rc=pltpu.VMEM(field, F32),
        t0=pltpu.VMEM(field, F32),
        t1=pltpu.VMEM(field, F32),
        pw=pltpu.VMEM(field, F32),
        gp=pltpu.VMEM(field, F32),
        gsum=pltpu.VMEM((2, N, N), F32),
        probe=pltpu.VMEM((3, 2, N, N), F32),
        dhi=pltpu.VMEM((2, N, 2 * N), BF16),
        dlo=pltpu.VMEM((2, N, 2 * N), BF16),
        lhi=pltpu.VMEM((2, 2 * N, N), BF16),
        llo=pltpu.VMEM((2, 2 * N, N), BF16),
        gbuf=pltpu.VMEM((2, N, 2 * N), F32),
        rbuf=pltpu.VMEM((2, 2 * N, N), F32),
        psi=pltpu.VMEM((2, 2 * N, N), F32),
        meas=pltpu.VMEM((2, N, N), F32),
        mats=pltpu.VMEM((4, 2, 2, N, N), BF16),
        perm=pltpu.VMEM((2, N, N), BF16),
        stage=pltpu.VMEM((2, N, N), F32),
        result=pltpu.VMEM(field, F32),
        r0=pltpu.VMEM((2, N, N), F32),
        r1=pltpu.VMEM((2, nx, xr, N), F32),
        r2=pltpu.VMEM((2, ny - 1, yr, N), F32),
        rz=pltpu.VMEM((2, nz, yr, N), F32),
        send=pltpu.SemaphoreType.DMA((copies,)),
        recv=pltpu.SemaphoreType.DMA((copies,)),
        local=pltpu.SemaphoreType.DMA((9,)),
    )
    return kernel, list(scratch.values())


def solution(mesh):
    n_ty, n_tx = mesh.shape["ty"], mesh.shape["tx"]
    kernel, scratch = make_kernel(n_ty, n_tx)
    mats, perm = tables(), shuffles()

    def body(object_planes, probe, positions, measured):
        return pl.pallas_call(
            kernel,
            out_shape=(
                jax.ShapeDtypeStruct(object_planes.shape, F32),
                jax.ShapeDtypeStruct(probe.shape, F32),
            ),
            in_specs=[pl.BlockSpec(memory_space=pltpu.SMEM)] + [pl.BlockSpec(memory_space=pl.ANY)] * 5,
            out_specs=(pl.BlockSpec(memory_space=pl.ANY), pl.BlockSpec(memory_space=pl.ANY)),
            scratch_shapes=scratch,
            compiler_params=pltpu.CompilerParams(
                collective_id=0, has_side_effects=True, vmem_limit_bytes=56 * 1024 * 1024),
        )(positions.reshape(4), object_planes, probe, measured[0, 0], jnp.asarray(mats), jnp.asarray(perm))

    return jax.shard_map(
        body,
        mesh=mesh,
        in_specs=(
            P(None, None, "ty", "tx"),
            P(),
            P("ty", "tx", None, None),
            P("ty", "tx", None, None, None),
        ),
        out_specs=(P(None, None, "ty", "tx"), P()),
        check_vma=False,
    )
```

time: 982 us -> 151 us (0.15)
  waiting for transfers between devices: 643 us -> 0 us
  matrix products: 166 us -> 0 us
  Pallas kernels: 0 us -> 146 us
  local copies, waits for them, and re-layouts: 77.2 us -> 4.41 us
  other arithmetic: 31.6 us -> 0 us
  starting transfers between devices: 25.2 us -> 0 us
  loops' own time: 16.5 us -> 0 us
  between operations: 15.7 us -> 0.65 us
    psum x2 -> x0, waiting for transfers between devices: 511 us -> none  [body(): probe_sum = lax.psum(probe_gradient, ('ty', 'tx'))]
    dot_general x96 -> x0, matrix products: 166 us -> none  [exact_product(): jnp.matmul(left, right, precision=lax.Precision.HIGHEST, preferred_elemen...]
    pallas_call x0 -> x1, Pallas kernels: none -> 146 us  [body(): pl.pallas_call(kernel, out_shape=(jax.ShapeDtypeStruct(object_planes.shap...]
    ppermute x10 -> x0, waiting for transfers between devices: 133 us -> none  [from_behind(): return lax.ppermute(shard, axis, pairs)]
    dynamic_update_slice x4 -> x0, local copies, waits for them, and re-layouts: 48.4 us -> none  [add_patch(): return lax.dynamic_update_slice(grad_ext, old + grad_patches[index], start)]
    ppermute x10 -> x0, starting transfers between devices: 25.1 us -> none  [from_behind(): return lax.ppermute(shard, axis, pairs)]
    another operation x4 -> x0, loops' own time: 16.5 us -> none  [the longest x2 15.5 us: body(): grad_ext = lax.fori_loop(0, count_dev, add_patch, jnp.zeros_like(extended))]
    gather x12 -> x0, local copies, waits for them, and re-layouts: 15.1 us -> none
  transfers between devices with their start and end apart: 12 -> 0, of which waited for: 7 -> 0; matrix products, arithmetic and copies ran while one was open for 1% -> 0% of each run, Pallas kernels for 0% -> 0%
where the time goes in v1:
time: 151 us
  Pallas kernels  146 us (97%)
  local copies, waits for them, and re-layouts  4.41 us (3%)
    pallas_call x1, Pallas kernels, body(): pl.pallas_call(kernel, out_shape=(jax.ShapeDtypeStruct(object_planes.shap...  146 us
    unnamed x4, local copies, waits for them, and re-layouts  3.14 us

profile of v1, /device:TPU:1, one launch (start us, length us, event | category | flops | bytes accessed | tf_op | source)
XLA Modules:
  0.0 151.0 jit_solution(14628830148878421648)
XLA Ops:
  0.6 1.3 reshape.7.pos
  1.9 145.9 %shard_map.77 = (f32[2,2,256,256]{3,2,1,0:T(8,128)}, f32[2,256,256]{2,1,0:T(8,128)}) custom-call(s32[4]{0:T(128)} %reshape.7.pos, f32[2,2,256,256]{3,2,1,0:T(8,128)} %obj.1, f32[2,256,256]{2,1,0:T(8,128)} %probe_in.1, f32[2,256,256]{2,1,0:T(8,128)} %bitcast.1, bf16[4,2,2,256,256]{4,3,2,1,0:T(8,128)(2,1)} %constant.4.clone.mats_in, ...), custom_call_target="tpu_custom_call" | custom-call | tf_op jit(solution)/shard_map/pallas_call | solution.py:634
  147.8 0.0 copy-start
  147.8 2.3 %copy.10 = f32[2,2,256,256]{3,2,1,0:T(8,128)} copy(f32[2,2,256,256]{3,2,1,0:T(8,128)} %get-tuple-element.4) | data formatting | bytes 2097152
  150.2 0.0 copy-done
  150.2 0.8 copy.11
Async XLA Ops:
  147.8 2.4 %copy-start = (f32[2,256,256]{2,1,0:T(8,128)S(1)}, f32[2,256,256]{2,1,0:T(8,128)}, u32[]{:S(2)}) copy-start(f32[2,256,256]{2,1,0:T(8,128)} %get-tuple-element.5) | copy-start | bytes 1572868

commit v2 on v1

--- a/solution.py
+++ b/solution.py
@@ -16,8 +16,16 @@
 H = 128
 ITERS = 2
 RB = 16
-CHUNKS = [(s, p, h * H, H) for s in (1, 0) for p in (0, 1) for h in (0, 1)]
-NCH = len(CHUNKS)
+CR = 64
+QUARTERS = N // CR
+GATHER = [(0, 0), (0, 1), (1, 0), (1, 1)]
+MID = [(1, 0), (0, 0), (0, 1), (1, 1)]
+LAST = [(1, 0), (1, 1), (0, 0), (0, 1)]
+NCH = 4 * QUARTERS
+SENDERS = 24
+ARRIVALS = 112
+MID_PLAN = ("r", "A2", "r", "A4", "B2", "r", "r", "A3", "B4", "C3", "r", "A3", "B4", "C3", "r", "B4", "C4", "r", "B2", "C3", "r", "C1")
+END_PLAN = ("r", "B3", "r", "B3", "r", "B2", "K8", "r", "B2", "r", "L8", "B2", "r", "B2", "r", "B2", "L8", "r", "E4", "r", "E4", "r", "E8")
 OBJ_STEP = 0.1
 
 
@@ -89,7 +97,7 @@
         body(pl.multiple_of(b * RB, RB))
         return carry
 
-    lax.fori_loop(0, count, step, 0)
+    lax.fori_loop(0, count, step, 0, unroll=True)
 
 
 def make_kernel(n_ty, n_tx):
@@ -97,12 +105,12 @@
     nx = n_tx // ny
     nz = n_ty // 2
     xr = N // nx
-    yr = xr // ny
+    zr = xr // nz
 
     def kernel(pos, obj, probe_in, meas_in, mats_in, perm_in, obj_out, probe_out,
                tor, tbc1, tbc2, gor, gbc, ra, rb, rc, t0, t1, pw, gp, gsum, probe,
                dhi, dlo, lhi, llo, gbuf, rbuf, psi, meas, mats, perm, stage, result,
-               r0, r1, r2, rz, send, recv, local):
+               r0, r1, r2, ry, send, recv, local):
         ty = lax.axis_index("ty")
         tx = lax.axis_index("tx")
         up = (lax.rem(ty + n_ty - 1, n_ty), tx)
@@ -122,18 +130,24 @@
         has_left = jnp.where(tx > 0, 1.0, 0.0).astype(F32)
         has_right = jnp.where(tx < n_tx - 1, 1.0, 0.0).astype(F32)
 
-        used = [0]
-
-        def remote(src, dst, device):
-            index = used[0]
-            used[0] += 1
+        senders, arrivals = iter(range(SENDERS)), iter(range(ARRIVALS))
+
+        def remote(src, dst, device, out, into):
             return pltpu.make_async_remote_copy(
-                src_ref=src, dst_ref=dst, send_sem=send.at[index], recv_sem=recv.at[index],
+                src_ref=src, dst_ref=dst, send_sem=send.at[out], recv_sem=recv.at[into],
                 device_id=device, device_id_type=MESH)
 
-        def rows_of(chunk):
-            s, p, r, n = chunk
-            return s, p, pl.ds(r, n)
+        def landed(ref, into):
+            pltpu.make_async_copy(ref, ref, recv.at[into]).wait()
+
+        def gone(ref, out):
+            pltpu.make_async_copy(ref, ref, send.at[out]).wait()
+
+        def take(source, count):
+            return [next(source) for _ in range(count)]
+
+        def chunks(order):
+            return [(s, p, pl.ds(r * CR, CR)) for s, p in order for r in range(QUARTERS)]
 
         loads = [
             pltpu.make_async_copy(obj.at[1], stage, local.at[0]),
@@ -141,7 +155,7 @@
             pltpu.make_async_copy(obj.at[0], tor.at[0, 0], local.at[2]),
             pltpu.make_async_copy(probe_in, probe.at[0], local.at[3]),
             pltpu.make_async_copy(mats_in, mats, local.at[4]),
-            pltpu.make_async_copy(meas_in, meas, local.at[5]),
+            pltpu.make_async_copy(meas_in.at[0, 0], meas, local.at[5]),
         ]
         for copy in loads:
             copy.start()
@@ -152,14 +166,14 @@
             pl.semaphore_signal(barrier, inc=1, device_id=device, device_id_type=MESH)
         pl.semaphore_wait(barrier, len(partners))
 
-        first_chunks = CHUNKS[NCH // 2:] + CHUNKS[:NCH // 2]
         own_left, own_up, right_up = [], [], []
-        for chunk in first_chunks:
-            s, p, rows = rows_of(chunk)
+        out_left, out_up, out_right = take(senders, 3)
+        in_right, in_below, in_corner = take(arrivals, NCH), take(arrivals, 2), take(arrivals, 2)
+        for i, (s, p, rows) in enumerate(chunks(GATHER)):
             src = obj.at[0, p, rows] if s == 0 else tor.at[0, 1, p, rows]
-            own_left.append(remote(src, tor.at[1, s, p, rows], left))
-            own_up.append(remote(src, tbc1.at[0, s, p, rows], up))
-            right_up.append(remote(tor.at[1, s, p, rows], tbc1.at[1, s, p, rows], up))
+            own_left.append(remote(src, tor.at[1, s, p, rows], left, out_left, in_right[i]))
+            own_up.append(remote(src, tbc1.at[0, s, p, rows], up, out_up, in_below[s]))
+            right_up.append(remote(tor.at[1, s, p, rows], tbc1.at[1, s, p, rows], up, out_right, in_corner[s]))
         for i in range(NCH // 2):
             own_left[i].start()
             own_up[i].start()
@@ -167,7 +181,7 @@
         loads[1].wait()
         for p in (0, 1):
             tor[0, 1, p] = permute_cols(perm[1], permute_rows(perm[0], stage[p]))
-            for i in range(NCH // 2 + p * NCH // 4, NCH // 2 + (p + 1) * NCH // 4):
+            for i in range((2 + p) * QUARTERS, (3 + p) * QUARTERS):
                 own_left[i].start()
                 own_up[i].start()
 
@@ -177,7 +191,7 @@
         row_half = lax.broadcasted_iota(jnp.int32, (RB, H), 0)
         row_sign = jnp.where(lax.rem(row_in_block, 2) == 1, -1.0, 1.0).astype(F32)
         col_sign = jnp.where(lax.rem(col_half, 2) == 1, -1.0, 1.0).astype(F32)
-        offsets = [(pos[0], pos[1]), (pos[2], pos[3])]
+        offsets = [(pos[0, 0, 0, 0], pos[0, 0, 0, 1]), (pos[0, 0, 1, 0], pos[0, 0, 1, 1])]
 
         def window(tbc, s, p, rows, cols, row_ok, col_ok):
             upper = jnp.where(col_ok, tor[0, s, p, rows, cols], has_right * tor[1, s, p, rows, cols])
@@ -241,7 +255,7 @@
                     moved = pltpu.roll(probe[step, k], offsets[q][0], 0)
                     pw[q, k] = pltpu.roll(moved, offsets[q][1], 1)
 
-        def forward_first(tbc):
+        def forward_first(tbc, pump=lambda: None):
             def body(rr):
                 for q in (0, 1):
                     r, c = offsets[q]
@@ -261,8 +275,11 @@
                         put_d(0, rr, k, pl.ds(q * N, N), fields[0][k] + high)
                         put_d(1, rr, k, pl.ds(q * N, N), fields[0][k] - high)
             blocks(H // RB, body)
+            pump()
             left_product(0)
+            pump()
             col_split(True)
+            pump()
             right_product(1, psi)
 
         def forward_rest(tbc):
@@ -374,218 +391,249 @@
                     parts.append(pltpu.roll(back, lax.rem(N - offsets[q][1], N), 1))
                 gsum[k] = parts[0] + parts[1]
 
-        def reduction(step):
+        def reduction(step, ring):
             buf = step
-            c0 = remote(gsum.at[1 - core], r0.at[buf], mate)
+            o0, o1, o2, o3, o4, o5, o6 = take(senders, 7)
+            i0, i1, i2, i4, i5, i6 = take(arrivals, 6)
+            i3 = take(arrivals, ny - 1 if ring else 1)
+            c0 = remote(gsum.at[1 - core], r0.at[buf], mate, o0, i0)
             c1 = [remote(r0.at[buf, pl.ds(pl.multiple_of(lax.rem(x + d, nx) * xr, xr), xr)],
-                         r1.at[buf, d - 1], xs[d - 1]) for d in range(1, nx)]
-            c2 = [remote(r1.at[buf, nx - 1, pl.ds(pl.multiple_of(lax.rem(y + d, ny) * yr, yr), yr)],
-                         r2.at[buf, d - 1], ys[d - 1]) for d in range(1, ny)]
-            c3 = [remote(rz.at[buf, z], rz.at[buf, z], zs[d - 1]) for d in range(1, nz)]
+                         r1.at[buf, d - 1], xs[d - 1], o1, i1) for d in range(1, nx)]
+            c2 = [remote(r1.at[buf, nx - 1, pl.ds(pl.multiple_of(lax.rem(z + d, nz) * zr, zr), zr)],
+                         r2.at[buf, d - 1], zs[d - 1], o2, i2) for d in range(1, nz)]
+            if ring:
+                slots = [ry.at[buf, lax.rem(y + d, ny)] for d in range(ny - 1)]
+                c3 = [remote(slot, slot, ys[-1], o3, i3[d]) for d, slot in enumerate(slots)]
+            else:
+                c3 = [remote(ry.at[buf, y], ry.at[buf, y], ys[d - 1], o3, i3[0]) for d in range(1, ny)]
+            all_x, all_z = r1.at[buf, pl.ds(0, nx - 1)], r2.at[buf]
+            all_y = ry.at[buf, pl.ds(0, ny - 1)]
             base_x = pl.multiple_of(x * xr, xr)
-            base_y = pl.multiple_of(y * yr, yr)
-            base = pl.multiple_of(x * xr + y * yr, yr)
-            mine = probe.at[step + 1, core, pl.ds(base, yr)]
+            base_z = pl.multiple_of(z * zr, zr)
+            base = pl.multiple_of(x * xr + z * zr, zr)
+            mine = probe.at[step + 1, core, pl.ds(base, zr)]
             strip = probe.at[step + 1, core, pl.ds(base_x, xr)]
             plane = probe.at[step + 1, core]
-            c4 = [remote(mine, mine, ys[d - 1]) for d in range(1, ny)]
-            c5 = [remote(strip, strip, xs[d - 1]) for d in range(1, nx)]
-            c6 = remote(plane, plane, mate)
+            c4 = [remote(mine, mine, zs[d - 1], o4, i4) for d in range(1, nz)]
+            c5 = [remote(strip, strip, xs[d - 1], o5, i5) for d in range(1, nx)]
+            c6 = remote(plane, plane, mate, o6, i6)
 
             def a0():
                 c0.start()
 
             def a1():
-                c0.wait_recv()
+                landed(r0.at[buf], i0)
                 r0[buf] = r0[buf] + gsum[core]
                 for c in c1:
                     c.start()
 
             def a2():
                 total = r0[buf, pl.ds(base_x, xr)]
-                for i, c in enumerate(c1):
-                    c.wait_recv()
+                landed(all_x, i1)
+                for i in range(nx - 1):
                     total = total + r1[buf, i]
                 r1[buf, nx - 1] = total
                 for c in c2:
                     c.start()
 
             def a3():
-                total = r1[buf, nx - 1, pl.ds(base_y, yr)]
-                for i, c in enumerate(c2):
-                    c.wait_recv()
+                total = r1[buf, nx - 1, pl.ds(base_z, zr)]
+                landed(all_z, i2)
+                for i in range(nz - 1):
                     total = total + r2[buf, i]
-                rz[buf, z] = total
-                for c in c3:
+                ry[buf, y] = total
+                for c in c3[:1] if ring else c3:
                     c.start()
 
+            def next_hop(i):
+                landed(ry.at[buf, 0], i3[i - 1])
+                c3[i].start()
+
+            hops = [(lambda i=i: next_hop(i)) for i in range(1, ny - 1)] if ring else []
+
             def a4():
-                for c in c3:
-                    c.wait_recv()
-                total = rz[buf, 0]
-                for i in range(1, nz):
-                    total = total + rz[buf, i]
+                landed(ry.at[buf, 0] if ring else all_y, i3[-1])
+                total = ry[buf, 0]
+                for i in range(1, ny):
+                    total = total + ry[buf, i]
                 scale = 0.5 / (n_ty * n_tx * 2)
-                probe[step + 1, core, pl.ds(base, yr)] = probe[step, core, pl.ds(base, yr)] - scale * total
+                probe[step + 1, core, pl.ds(base, zr)] = probe[step, core, pl.ds(base, zr)] - scale * total
                 for c in c4:
                     c.start()
 
             def a5():
-                for c in c4:
-                    c.wait_recv()
+                landed(all_z, i4)
                 for c in c5:
                     c.start()
 
             def a6():
-                for c in c5:
-                    c.wait_recv()
+                landed(all_x, i5)
                 c6.start()
 
             def a7():
-                c6.wait_recv()
-                for c in [c0, c6] + c1 + c2 + c3 + c4 + c5:
-                    c.wait_send()
-
-            return [a0, a1, a2, a3, a4, a5, a6, a7]
-
-        def grads_down(step):
-            return [remote(gbc.at[:, s, p, rows], ra.at[step, :, s, p, rows], down)
-                    for s, p, rows in map(rows_of, CHUNKS)]
+                landed(r0.at[buf], i6)
+                for ref, out in ((r0.at[buf], o0), (all_x, o1), (all_z, o2), (all_y, o3),
+                                 (all_z, o4), (all_x, o5), (r0.at[buf], o6)):
+                    gone(ref, out)
+
+            return [a0, a1, a2, a3] + hops + [a4, a5, a6, a7]
+
+        def add_above(part, place, step):
+            s, p, rows = place
+            gor[part, s, p, rows] = gor[part, s, p, rows] + has_above * ra[step, part, s, p, rows]
+
+        def act(i):
+            if i < len(actions):
+                actions[i]()
+
+        def follow(plan, steps):
+            done = dict.fromkeys(steps, 0)
+            for word in plan:
+                for _ in range(int(word[1:] or 1)):
+                    steps[word[0]](done[word[0]])
+                    done[word[0]] += 1
 
         half = NCH // 2
-        for i in range(half):
-            own_left[i].wait_recv()
-            right_up[i].start()
+        early = half + 2
+
+        def relay(first, last):
+            for i in range(first, last):
+                s, p, rows = chunks(GATHER)[i]
+                landed(tor.at[1, s, p, rows], in_right[i])
+                right_up[i].start()
+
+        relay(0, half)
         loads[2].wait()
         loads[3].wait()
         roll_probe(0)
-        own_left[half].wait_recv()
-        right_up[half].start()
-        for i in range(half):
-            own_up[i].wait_recv()
-            right_up[i].wait_recv()
+        relay(half, early)
+        landed(tbc1.at[0, 0], in_below[0])
+        landed(tbc1.at[1, 0], in_corner[0])
         loads[4].wait()
-        forward_first(tbc1)
-        for i in range(half + 1, NCH):
-            own_left[i].wait_recv()
-            right_up[i].start()
-        for i in range(half, NCH):
-            own_up[i].wait_recv()
-            right_up[i].wait_recv()
+        at = [early]
+
+        def pump_gather():
+            if at[0] < NCH:
+                relay(at[0], at[0] + 1)
+                at[0] += 1
+
+        forward_first(tbc1, pump_gather)
+        relay(at[0], NCH)
+        landed(tbc1.at[0, 1], in_below[1])
+        landed(tbc1.at[1, 1], in_corner[1])
         loads[5].wait()
         forward_rest(tbc1)
         backward_first()
         backward_second()
-        for c in own_left + own_up + right_up:
-            c.wait_send()
-
-        a_sends = grads_down(0)
-        b_right, b_left, c_up = [], [], []
-        for s, p, rows in map(rows_of, CHUNKS):
-            b_right.append(remote(gor.at[1, s, p, rows], rb.at[0, s, p, rows], right))
-            b_left.append(remote(gor.at[0, s, p, rows], rc.at[s, p, rows], left))
-            c_up.append(remote(tor.at[:, s, p, rows], tbc2.at[:, s, p, rows], up))
-        for i in range(half):
-            a_sends[i].start()
+        gone(tor.at[0], out_left)
+        gone(tor.at[0], out_up)
+        gone(tor.at[1], out_right)
+
+        places = chunks(MID)
+        out_a, out_right, out_left, out_up = take(senders, 4)
+        in_a, in_b, in_up = take(arrivals, NCH), take(arrivals, NCH), take(arrivals, 2)
+        a_sends, b_right, b_left, c_up = [], [], [], []
+        for i, (s, p, rows) in enumerate(places):
+            a_sends.append([remote(gbc.at[part, s, p, rows], ra.at[0, part, s, p, rows], down, out_a, in_a[i])
+                            for part in (0, 1)])
+            b_right.append(remote(gor.at[1, s, p, rows], rb.at[0, s, p, rows], right, out_right, in_b[i]))
+            b_left.append(remote(gor.at[0, s, p, rows], rb.at[1, s, p, rows], left, out_left, in_b[i]))
+            c_up.append(remote(tor.at[:, s, p, rows], tbc2.at[:, s, p, rows], up, out_up, in_up[s]))
+        for i in range(QUARTERS):
+            for c in a_sends[i]:
+                c.start()
         backward_last()
-        for i in range(half, NCH):
-            a_sends[i].start()
         sum_probe()
-        actions = reduction(0)
-        actions.pop(0)()
-
-        def add_above(i, step):
-            s, p, rows = rows_of(CHUNKS[i])
-            a_sends[i].wait_recv()
+        actions = reduction(0, False)
+
+        def mid_a(i):
+            for c in a_sends[QUARTERS + i]:
+                c.start()
+
+        def mid_b(i):
+            s, p, rows = places[i]
+            landed(ra.at[0, :, s, p, rows], in_a[i])
             for part in (0, 1):
-                gor[part, s, p, rows] = gor[part, s, p, rows] + has_above * ra[step, part, s, p, rows]
-
-        def mid_b(i):
-            add_above(i, 0)
+                add_above(part, places[i], 0)
             b_right[i].start()
             b_left[i].start()
 
         def mid_c(i):
-            s, p, rows = rows_of(CHUNKS[i])
-            b_right[i].wait_recv()
-            b_left[i].wait_recv()
+            s, p, rows = places[i]
+            landed(rb.at[:, s, p, rows], in_b[i])
             tor[0, s, p, rows] = tor[0, s, p, rows] - OBJ_STEP * (
                 gor[0, s, p, rows] + has_left * rb[0, s, p, rows])
             tor[1, s, p, rows] = tor[1, s, p, rows] - OBJ_STEP * (
-                gor[1, s, p, rows] + has_right * rc[s, p, rows])
+                gor[1, s, p, rows] + has_right * rb[1, s, p, rows])
             c_up[i].start()
 
-        mid_b(0)
-        for i in range(1, NCH):
-            mid_b(i)
-            mid_c(i - 1)
-            if actions:
-                actions.pop(0)()
-        mid_c(NCH - 1)
-        while actions:
-            actions.pop(0)()
+        follow(MID_PLAN, dict(r=act, A=mid_a, B=mid_b, C=mid_c))
         roll_probe(1)
-        for c in c_up:
-            c.wait_recv()
-        for c in a_sends + b_right + b_left:
-            c.wait_send()
-
-        forward_first(tbc2)
+        landed(tbc2.at[:, 0], in_up[0])
+        gone(gbc, out_a)
+
+        at[0] = NCH - 2
+
+        def pump_mid():
+            if at[0] < NCH:
+                mid_c(at[0])
+                at[0] += 1
+
+        forward_first(tbc2, pump_mid)
+        gone(gor.at[1], out_right)
+        gone(gor.at[0], out_left)
+        landed(tbc2.at[:, 1], in_up[1])
         forward_rest(tbc2)
         backward_first()
         backward_second()
-        for c in c_up:
-            c.wait_send()
-        a_sends = grads_down(1)
-        b_right = [remote(gor.at[1, s, p, rows], rb.at[1, s, p, rows], right)
-                   for s, p, rows in map(rows_of, CHUNKS)]
+        gone(tor, out_up)
+        places = chunks(LAST)
+        out_a, out_right = take(senders, 2)
+        in_a, in_b, in_below = take(arrivals, NCH), take(arrivals, NCH), take(arrivals, 4)
+        a_sends, b_right = [], []
+        for i, (s, p, rows) in enumerate(places):
+            a_sends.append([remote(gbc.at[part, s, p, rows], ra.at[1, part, s, p, rows], down, out_a,
+                                   in_a[i] if part else in_below[i // QUARTERS]) for part in (0, 1)])
+            b_right.append(remote(gor.at[1, s, p, rows], rc.at[s, p, rows], right, out_right, in_b[i]))
         for i in range(half):
-            a_sends[i].start()
+            a_sends[i][1].start()
         backward_last()
-        for i in range(half, NCH):
-            a_sends[i].start()
         sum_probe()
-        actions = reduction(1)
-        actions.pop(0)()
+        actions = reduction(1, True)
 
         def end_b(i):
-            add_above(i, 1)
+            s, p, rows = places[i]
+            landed(ra.at[1, 1, s, p, rows], in_a[i])
+            add_above(1, places[i], 1)
             b_right[i].start()
 
         def end_c(i):
-            s, p, rows = rows_of(CHUNKS[i])
-            b_right[i].wait_recv()
-            value = tor[0, s, p, rows] - OBJ_STEP * (gor[0, s, p, rows] + has_left * rb[1, s, p, rows])
+            s, p, rows = places[i]
+            if i % QUARTERS == 0:
+                landed(ra.at[1, 0, s, p], in_below[i // QUARTERS])
+            landed(rc.at[s, p, rows], in_b[i])
+            value = tor[0, s, p, rows] - OBJ_STEP * (
+                gor[0, s, p, rows] + has_above * ra[1, 0, s, p, rows] + has_left * rc[s, p, rows])
             if s == 0:
                 result[0, p, rows] = value
             else:
                 stage[p, rows] = value
+            if i % QUARTERS == QUARTERS - 1:
+                if s == 1:
+                    result[1, p] = permute_cols(perm[0], permute_rows(perm[1], stage[p]))
+                stores.append(pltpu.make_async_copy(result.at[s, p], obj_out.at[s, p], local.at[6 + len(stores)]))
+                stores[-1].start()
 
         stores = []
-        end_b(0)
-        for i in range(1, NCH):
-            end_b(i)
-            end_c(i - 1)
-            if actions:
-                actions.pop(0)()
-            if i == half + 1:
-                for p in (0, 1):
-                    result[1, p] = permute_cols(perm[0], permute_rows(perm[1], stage[p]))
-                stores.append(pltpu.make_async_copy(result.at[1], obj_out.at[1], local.at[6]))
-                stores[-1].start()
-        end_c(NCH - 1)
-        stores.append(pltpu.make_async_copy(result.at[0], obj_out.at[0], local.at[7]))
+        follow(END_PLAN, dict(r=act, K=lambda i: a_sends[half + i][1].start(),
+                              L=lambda i: a_sends[i][0].start(), B=end_b, E=end_c))
+        stores.append(pltpu.make_async_copy(probe.at[2], probe_out, local.at[10]))
         stores[-1].start()
-        while actions:
-            actions.pop(0)()
-        stores.append(pltpu.make_async_copy(probe.at[2], probe_out, local.at[8]))
-        stores[-1].start()
-        for c in a_sends + b_right:
-            c.wait_send()
+        gone(gbc, out_a)
+        gone(gor.at[1], out_right)
         for copy in stores:
             copy.wait()
 
-    copies = 3 * NCH + 4 * NCH + 2 * NCH + 2 * (2 + 2 * (nx - 1) + 2 * (ny - 1) + nz - 1)
     field = (2, 2, N, N)
     scratch = dict(
         tor=pltpu.VMEM((2,) + field, F32),
@@ -616,13 +664,33 @@
         result=pltpu.VMEM(field, F32),
         r0=pltpu.VMEM((2, N, N), F32),
         r1=pltpu.VMEM((2, nx, xr, N), F32),
-        r2=pltpu.VMEM((2, ny - 1, yr, N), F32),
-        rz=pltpu.VMEM((2, nz, yr, N), F32),
-        send=pltpu.SemaphoreType.DMA((copies,)),
-        recv=pltpu.SemaphoreType.DMA((copies,)),
-        local=pltpu.SemaphoreType.DMA((9,)),
+        r2=pltpu.VMEM((2, nz - 1, zr, N), F32),
+        ry=pltpu.VMEM((2, ny, zr, N), F32),
+        send=pltpu.SemaphoreType.DMA((SENDERS,)),
+        recv=pltpu.SemaphoreType.DMA((ARRIVALS,)),
+        local=pltpu.SemaphoreType.DMA((11,)),
     )
     return kernel, list(scratch.values())
+
+
+def publish(planes, probe):
+    def kernel(planes_in, probe_in, planes_out, probe_out, sems):
+        copies = [pltpu.make_async_copy(planes_in.at[s, p], planes_out.at[s, p], sems.at[2 * s + p])
+                  for s in (0, 1) for p in (0, 1)]
+        copies.append(pltpu.make_async_copy(probe_in, probe_out, sems.at[4]))
+        for copy in copies:
+            copy.start()
+        for copy in copies:
+            copy.wait()
+
+    anywhere = pl.BlockSpec(memory_space=pl.ANY)
+    return pl.pallas_call(
+        kernel,
+        out_shape=(jax.ShapeDtypeStruct(planes.shape, F32), jax.ShapeDtypeStruct(probe.shape, F32)),
+        in_specs=[pl.BlockSpec(memory_space=pltpu.VMEM)] * 2,
+        out_specs=(anywhere, anywhere),
+        scratch_shapes=[pltpu.SemaphoreType.DMA((5,))],
+    )(planes, probe)
 
 
 def solution(mesh):
@@ -631,7 +699,7 @@
     mats, perm = tables(), shuffles()
 
     def body(object_planes, probe, positions, measured):
-        return pl.pallas_call(
+        found = pl.pallas_call(
             kernel,
             out_shape=(
                 jax.ShapeDtypeStruct(object_planes.shape, F32),
@@ -642,7 +710,8 @@
             scratch_shapes=scratch,
             compiler_params=pltpu.CompilerParams(
                 collective_id=0, has_side_effects=True, vmem_limit_bytes=56 * 1024 * 1024),
-        )(positions.reshape(4), object_planes, probe, measured[0, 0], jnp.asarray(mats), jnp.asarray(perm))
+        )(positions, object_planes, probe, measured, jnp.asarray(mats), jnp.asarray(perm))
+        return publish(*found)
 
     return jax.shard_map(
         body,

time: 151 us -> 134 us (0.89)
  Pallas kernels: 146 us -> 133 us
  local copies, waits for them, and re-layouts: 4.41 us -> 0 us
    pallas_call x1, Pallas kernels: 146 us -> 131 us  [body(): pl.pallas_call(kernel, out_shape=(jax.ShapeDtypeStruct(object_planes.shap...]
    unnamed x4 -> x0, local copies, waits for them, and re-layouts: 3.14 us -> none
    pallas_call x0 -> x1, Pallas kernels: none -> 2.54 us  [publish(): pl.pallas_call(kernel, out_shape=(jax.ShapeDtypeStruct(planes.shape, F32)...]
where the time goes in v2:
time: 134 us
  Pallas kernels  133 us (99%)
    pallas_call x1, Pallas kernels, body(): pl.pallas_call(kernel, out_shape=(jax.ShapeDtypeStruct(object_planes.shap...  131 us

profile of v2, /device:TPU:1, one launch (start us, length us, event | category | flops | bytes accessed | tf_op | source)
XLA Modules:
  0.0 134.1 jit_solution(7748976424009874215)
XLA Ops:
  0.6 130.8 %shard_map.77 = (f32[2,2,256,256]{3,2,1,0:T(8,128)}, f32[2,256,256]{2,1,0:T(8,128)}) custom-call(s32[1,1,2,2]{3,2,1,0:T(2,128)} %pos.1, f32[2,2,256,256]{3,2,1,0:T(8,128)} %obj.1, f32[2,256,256]{2,1,0:T(8,128)} %probe_in.1, f32[1,1,2,256,256]{4,3,2,1,0:T(8,128)} %meas_in.1, bf16[4,2,2,256,256]{4,3,2,1,0:T(8,128)(2,1)} %constant.4.clone.mats_in, ...), custom_call_target="tpu_custom_call" | custom-call | tf_op jit(solution)/shard_map/pallas_call | solution.py:702
  131.4 2.5 %shard_map.78 = (f32[2,2,256,256]{3,2,1,0:T(8,128)}, f32[2,256,256]{2,1,0:T(8,128)}) custom-call(f32[2,2,256,256]{3,2,1,0:T(8,128)} %get-tuple-element.4.planes_in, f32[2,256,256]{2,1,0:T(8,128)} %get-tuple-element.5.probe_in), custom_call_target="tpu_custom_call" | custom-call | tf_op jit(solution)/shard_map/pallas_call | solution.py:687

commit v3 on v2

--- a/solution.py
+++ b/solution.py
@@ -24,8 +24,8 @@
 NCH = 4 * QUARTERS
 SENDERS = 24
 ARRIVALS = 112
-MID_PLAN = ("r", "A2", "r", "A4", "B2", "r", "r", "A3", "B4", "C3", "r", "A3", "B4", "C3", "r", "B4", "C4", "r", "B2", "C3", "r", "C1")
-END_PLAN = ("r", "B3", "r", "B3", "r", "B2", "K8", "r", "B2", "r", "L8", "B2", "r", "B2", "r", "B2", "L8", "r", "E4", "r", "E4", "r", "E8")
+MID_PLAN = ("r", "A2", "r", "A4", "B2", "r", "A3", "B3", "r", "B3", "C3", "A3", "r", "B3", "C3", "r", "B3", "C3", "r", "B2", "C3", "r", "C2")
+END_PLAN = ("r", "r", "B4", "r", "K8", "B4", "r", "L8", "B2", "r", "B3", "r", "B3", "r", "L8", "r", "E4", "r", "E4", "r", "E8")
 OBJ_STEP = 0.1
 
 

time: 134 us -> 129 us (0.963)
  Pallas kernels: 133 us -> 128 us
    pallas_call x1, Pallas kernels: 131 us -> 126 us  [body(): pl.pallas_call(kernel, out_shape=(jax.ShapeDtypeStruct(object_planes.shap...]
where the time goes in v3:
time: 129 us
  Pallas kernels  128 us (99%)
    pallas_call x1, Pallas kernels, body(): pl.pallas_call(kernel, out_shape=(jax.ShapeDtypeStruct(object_planes.shap...  126 us

profile of v3, /device:TPU:1, one launch (start us, length us, event | category | flops | bytes accessed | tf_op | source)
XLA Modules:
  0.0 129.1 jit_solution(1588577183665556525)
XLA Ops:
  0.6 125.7 %shard_map.77 = (f32[2,2,256,256]{3,2,1,0:T(8,128)}, f32[2,256,256]{2,1,0:T(8,128)}) custom-call(s32[1,1,2,2]{3,2,1,0:T(2,128)} %pos.1, f32[2,2,256,256]{3,2,1,0:T(8,128)} %obj.1, f32[2,256,256]{2,1,0:T(8,128)} %probe_in.1, f32[1,1,2,256,256]{4,3,2,1,0:T(8,128)} %meas_in.1, bf16[4,2,2,256,256]{4,3,2,1,0:T(8,128)(2,1)} %constant.4.clone.mats_in, ...), custom_call_target="tpu_custom_call" | custom-call | tf_op jit(solution)/shard_map/pallas_call | solution.py:702
  126.4 2.5 %shard_map.78 = (f32[2,2,256,256]{3,2,1,0:T(8,128)}, f32[2,256,256]{2,1,0:T(8,128)}) custom-call(f32[2,2,256,256]{3,2,1,0:T(8,128)} %get-tuple-element.4.planes_in, f32[2,256,256]{2,1,0:T(8,128)} %get-tuple-element.5.probe_in), custom_call_target="tpu_custom_call" | custom-call | tf_op jit(solution)/shard_map/pallas_call | solution.py:687
